TPU v7x, 32 devices: a whole 2x2x4 slice. The times are simulated.
32 devices in a mesh: ifg: 16 (over z, y, x), tile: 2 (over core).
Axes of the slice: x: 2, y: 2, z: 4, core: 2. Of those that a mesh axis runs over, the one named last changes fastest.
Arguments:
- phases: float32 [1024, 128, 64], P('ifg', 'tile'), may hold values from -6 to 6
- pairs: int32 [1024, 2], replicated, may hold values from 0 to 299, as said below
- class_weights: float32 [8, 1024], replicated, may hold values from 0.05 to 1
- classes: int32 [128, 64], P('tile', 'ifg'), may hold values from 0 to 7
Outputs:
- corrected: float32 [128, 64, 300], P('tile', 'ifg')
Inputs may be any that keep to these rules, and one draw needn't show every extreme that they name: pairs[i,0] < pairs[i,1] <= pairs[i,0] + 8; some interferogram starts at date 0 and some ends at date 300 - 1.
All inputs are finite; a program needn't handle non-finite values.
Results may differ from a plain program's by a relative error of at most 0.0003.
Values sent between devices are 32-bit elements; how exact they have to be, the bound alone decides.
A program may use at most 128 MiB of HBM per device.

v0:
```python
import jax
import jax.numpy as jnp
from jax import lax
from jax.sharding import PartitionSpec as P

DATES = 300
CLASSES = 8
MAXGAP = 8
R = 3
smooth_weight = 1.0
anchor_weight = 0.1


def with_halo(cells, sides, width):
    for axis, dim in sides:
        count = lax.axis_size(axis)
        ends = count - 1
        head = lax.slice_in_dim(cells, 0, width, axis=dim)
        tail = lax.slice_in_dim(cells, cells.shape[dim] - width, cells.shape[dim], axis=dim)
        cells = jnp.concatenate(
            [
                lax.ppermute(tail, axis, [(i, (i + 1) % count) for i in range(ends)]),
                cells,
                lax.ppermute(head, axis, [((i + 1) % count, i) for i in range(ends)]),
            ],
            axis=dim,
        )
    return cells


def incidence_matrix(pairs):
    dates = jnp.arange(DATES, dtype=jnp.int32)[:, None]
    plus = (dates == pairs[:, 1][None, :]).astype(jnp.float32)
    minus = (dates == pairs[:, 0][None, :]).astype(jnp.float32)
    return (plus, minus)


def prior_matrix():
    second = jnp.arange(DATES - 2, dtype=jnp.int32)[:, None]
    columns = jnp.arange(DATES, dtype=jnp.int32)[None, :]
    diffs = (
        (columns == second).astype(jnp.float32)
        - 2.0 * (columns == second + 1).astype(jnp.float32)
        + (columns == second + 2).astype(jnp.float32)
    )
    curvature = jnp.dot(
        diffs.T, diffs, precision=lax.Precision.HIGHEST, preferred_element_type=jnp.float32
    )
    return smooth_weight * curvature + anchor_weight * jnp.eye(DATES, dtype=jnp.float32)


def class_systems(pairs, plus, minus, weights):
    diagonal = jnp.dot(
        weights,
        (plus + minus).T,
        precision=lax.Precision.HIGHEST,
        preferred_element_type=jnp.float32,
    )
    spacing = pairs[:, 1] - pairs[:, 0]
    offsets = jnp.arange(1, MAXGAP + 1, dtype=jnp.int32)[:, None]
    gap_onehot = (spacing[None, :] == offsets).astype(jnp.float32)
    spread = weights[:, None, :] * gap_onehot[None, :, :]
    band = jnp.einsum("kgi,ai->kga", spread, minus, precision=lax.Precision.HIGHEST)
    row_ids = jnp.arange(DATES, dtype=jnp.int32)[:, None]
    col_ids = jnp.arange(DATES, dtype=jnp.int32)[None, :]
    normal = diagonal[:, :, None] * (row_ids == col_ids).astype(jnp.float32)[None]
    for offset in range(MAXGAP):
        select = (col_ids == row_ids + offset + 1).astype(jnp.float32)
        normal = (
            normal
            - band[:, offset, :, None] * select[None]
            - band[:, offset, None, :] * select.T[None]
        )
    return normal


def invert(matrix):
    factor = jnp.linalg.cholesky(matrix)
    return jax.scipy.linalg.cho_solve((factor, True), jnp.eye(DATES, dtype=jnp.float32))


def filter_taps():
    offsets = jnp.arange(-R, R + 1).astype(jnp.float32)
    values = jnp.exp(-offsets * offsets / 4.5)
    return values / jnp.sum(values)


def pass_columns(padded, filter_weights, width):
    result = filter_weights[0] * padded[:, 0:width]
    for offset in range(1, 2 * R + 1):
        result = result + filter_weights[offset] * padded[:, offset : offset + width]
    return result


def pass_rows(padded, filter_weights, height):
    result = filter_weights[0] * padded[0:height]
    for offset in range(1, 2 * R + 1):
        result = result + filter_weights[offset] * padded[offset : offset + height]
    return result


def date_terms(received, incidence, weight_rows, onehot):
    flat = received.reshape(received.shape[0], -1)
    pixel_weights = jnp.dot(
        weight_rows, onehot, precision=lax.Precision.HIGHEST, preferred_element_type=jnp.float32
    )
    return jnp.einsum("ip,di->pd", pixel_weights * flat, incidence, precision=lax.Precision.HIGHEST)


def on_device(phases, pairs, class_weights, classes):
    plus, minus = incidence_matrix(pairs)
    incidence = plus - minus
    class_share = CLASSES // lax.axis_size("tile")
    first_class = lax.axis_index("tile") * class_share
    own_weights = lax.dynamic_slice_in_dim(class_weights, first_class, class_share, 0)
    own_normal = class_systems(pairs, plus, minus, own_weights)
    own_inverse = jax.vmap(invert)(own_normal + prior_matrix()[None])
    inverse = lax.all_gather(own_inverse, "tile", axis=0, tiled=True)
    tile_rows = phases.shape[1]
    tile_cols = classes.shape[1]
    class_flat = classes.reshape(-1)
    onehot = (class_flat[None, :] == jnp.arange(CLASSES, dtype=jnp.int32)[:, None]).astype(
        jnp.float32
    )
    weight_rows = class_weights.T
    regrouped = lax.all_to_all(phases, "ifg", split_axis=2, concat_axis=0, tiled=True)
    right_terms = date_terms(regrouped, incidence, weight_rows, onehot)
    solution = jnp.zeros((tile_rows * tile_cols, DATES), jnp.float32)
    for member in range(CLASSES):
        solved = jnp.einsum(
            "pd,ed->pe", right_terms, inverse[member], precision=lax.Precision.HIGHEST
        )
        solution = solution + onehot[member][:, None] * solved
    displacement = solution.reshape(tile_rows, tile_cols, DATES)
    filter_weights = filter_taps()
    padded = with_halo(displacement, (("ifg", 1), ("tile", 0)), R)
    across = pass_columns(padded, filter_weights, tile_cols)
    atmosphere = pass_rows(across, filter_weights, tile_rows)
    return displacement - atmosphere


def solution(mesh):
    return jax.shard_map(
        on_device,
        mesh=mesh,
        in_specs=(P("ifg", "tile", None), P(), P(), P("tile", "ifg")),
        out_specs=P("tile", "ifg", None),
        check_vma=False,
    )
```

profile of v0, /device:TPU:13, one launch (start us, length us, event | category | flops | bytes accessed | tf_op | source)
XLA Modules:
  0.0 464.6 jit_solution(6404731645494615155)
XLA Ops:
  7.3 1.3 fusion.6
  9.5 1.4 bitcast_add_fusion
  12.6 4.8 %fusion.2 = f32[4,300,300]{2,1,0:T(8,128)S(1)} fusion(f32[300,300]{1,0:T(8,128)S(1)} %copy.75, f32[300,300]{1,0:T(8,128)S(1)} %copy.74, f32[4,300]{1,0:T(4,128)S(1)} %fusion.6, f32[300,300]{1,0:T(8,128)S(1)} %copy.73, f32[300,300]{1,0:T(8,128)S(1)} %get-tuple-element.96, f32[4,300]{1,0:T(4,128)S(1)} %get-tuple-element.82, ...), kind=kLoop, calls=%fused_computation.36 | loop fusion | flops 19440000 | bytes 8683200 | tf_op jit(solution)/shard_map/vmap(jit(cholesky))/div | solution.py:78
  17.4 1.3 copy-done.2
  18.7 46.9 %custom-call.29 = f32[4,128,128]{2,1,0:T(8,128)S(1)} custom-call(f32[4,128,128]{2,1,0:T(8,128)S(1)} %cholesky.205), custom_call_target="Cholesky" | custom-call | tf_op jit(solution)/shard_map/vmap(jit(cholesky))/cholesky | solution.py:78
  65.8 39.9 %custom-call.30 = f32[4,1,128,128]{2,3,1,0:T(8,128)} custom-call(f32[4,1,128,128]{3,2,1,0:T(8,128)S(1)} %select_bitcast_fusion.1), custom_call_target="InvertDiagBlocksLowerTriangular" | custom-call | tf_op jit(solution)/shard_map/vmap(jit(cholesky))/cholesky | solution.py:78
  105.7 1.5 constant_dynamic-update-slice_fusion.2
  107.2 1.7 convolution_subtract_fusion.3
  109.6 48.5 %custom-call.31 = f32[4,128,128]{2,1,0:T(8,128)} custom-call(f32[4,128,128]{2,1,0:T(8,128)} %cholesky.209), custom_call_target="Cholesky" | custom-call | tf_op jit(solution)/shard_map/vmap(jit(cholesky))/cholesky | solution.py:78
  158.1 1.7 select_reduce_fusion
  159.8 40.1 %custom-call.32 = f32[4,1,128,128]{2,3,1,0:T(8,128)S(1)} custom-call(f32[4,1,128,128]{3,2,1,0:T(8,128)} %get-tuple-element.31), custom_call_target="InvertDiagBlocksLowerTriangular" | custom-call | tf_op jit(solution)/shard_map/vmap(jit(cholesky))/cholesky | solution.py:78
  200.3 1.2 convolution_subtract_fusion.4
  201.5 16.1 %custom-call.33 = f32[4,44,44]{2,1,0:T(8,128)S(1)} custom-call(f32[4,44,44]{2,1,0:T(8,128)S(1)} %convolution_subtract_fusion.4), custom_call_target="Cholesky" | custom-call | tf_op jit(solution)/shard_map/vmap(jit(cholesky))/cholesky | solution.py:78
  218.9 1.8 select_select_fusion
  220.8 4.1 while.1
  221.4 1.4 bitcast_dynamic-update-slice_fusion.2
  223.5 1.4 bitcast_dynamic-update-slice_fusion.2
  225.1 118.7 %custom-call.34 = f32[4,3,128,128]{2,3,1,0:T(8,128)} custom-call(f32[4,3,128,128]{3,2,1,0:T(8,128)S(1)} %pad_maximum_fusion.2), custom_call_target="InvertDiagBlocksLowerTriangular" | custom-call | tf_op jit(solution)/shard_map/vmap(jit(_cho_solve))/triangular_solve | solution.py:79
  343.9 1.6 fusion.72
  346.2 1.6 fusion.81
  348.0 1.3 fusion.24
  349.2 1.3 fusion.92
  350.6 1.3 fusion.91
  351.9 2.0 convolution_subtract_fusion.1
  354.2 1.8 fusion.80
  356.0 1.2 convolution_subtract_fusion.2
  357.2 1.6 fusion.79
  359.0 1.8 copy.89
  360.8 3.1 copy.69
  363.9 2.3 reshape.539
  366.2 6.9 %all-to-all-start = ((f32[16,1,16384]{2,1,0:T(1,128)}), f32[16,1,16384]{2,1,0:T(1,128)S(1)}, u32[]{:S(2)}, u32[]{:S(2)}) async-start(f32[16,1,16384]{2,1,0:T(1,128)} %reshape.539), calls=%async_computation | async-start | bytes 2097152 | tf_op jit(solution)/shard_map/all_to_all | solution.py:126
  373.4 24.5 %all-to-all-done = f32[16,1,16384]{2,1,0:T(1,128)S(1)} async-done(((f32[16,1,16384]{2,1,0:T(1,128)}), f32[16,1,16384]{2,1,0:T(1,128)S(1)}, u32[]{:S(2)}, u32[]{:S(2)}) %all-to-all-start) | async-done | bytes 1048608 | tf_op jit(solution)/shard_map/all_to_all | solution.py:126
  398.4 3.1 reduce.18
  402.4 2.7 copy.70
  405.1 2.0 reshape.515
  407.8 1.4 fusion.5
  409.2 1.8 convolution_multiply_fusion.6
  411.0 1.7 convolution_multiply_fusion.5
  412.7 1.7 convolution_multiply_fusion.4
  414.4 1.7 convolution_multiply_fusion.3
  419.3 2.1 collective-permute-start
  421.5 4.1 collective-permute-start.1
  426.8 4.2 collective-permute-done
  431.0 10.1 %collective-permute-done.1 = f32[64,3,300]{2,1,0:T(4,128)S(1)} collective-permute-done((f32[64,3,300]{2,1,0:T(4,128)S(1)}, f32[64,3,300]{2,1,0:T(4,128)S(1)}, u32[]{:S(2)}, u32[]{:S(2)}) %collective-permute-start.1) | collective-permute-done | bytes 230432 | tf_op jit(solution)/shard_map/ppermute | solution.py:24
  441.1 1.3 collective-permute-start.2
  442.4 3.0 collective-permute-start.3
  446.8 5.0 %fusion.56 = f32[70,4,300]{2,1,0:T(4,128)S(1)} fusion(f32[70,10,300]{2,1,0:T(8,128)S(1)} %pad_maximum_fusion.1, f32[]{:T(128)} %bitcast.39, f32[]{:T(128)} %bitcast.38, f32[]{:T(128)} %bitcast.37, f32[]{:T(128)} %bitcast.36, f32[]{:T(128)} %bitcast.35, f32[]{:T(128)} %bitcast.34, f32[]{:T(128)} %bitcast.33), kind=kLoop, calls=%fused_computation.143 | loop fusion | flops 1092000 | bytes 2688028 | tf_op jit(solution)/shard_map/add | solution.py:91
  451.8 5.5 %fusion.63 = f32[64,4,300]{2,1,0:T(4,128)} fusion(f32[64,4,300]{2,1,0:T(4,128)S(1)} %reshape.516, f32[70,4,300]{2,1,0:T(4,128)S(1)} %fusion.56, f32[]{:T(128)} %bitcast.39, f32[]{:T(128)} %bitcast.38, f32[]{:T(128)} %bitcast.37, f32[]{:T(128)} %bitcast.36, f32[]{:T(128)} %bitcast.35, f32[]{:T(128)} %bitcast.34, f32[]{:T(128)} %bitcast.33), kind=kLoop, calls=%fused_computation.157 | loop fusion | flops 1075200 | bytes 2764828 | tf_op jit(solution)/shard_map/sub | solution.py:139
  (102 shorter events, 16.3 us)
Async XLA Ops:
  6.5 0.8 copy-start
  6.5 0.7 copy-start.5
  6.5 402.6 %all-gather.2.cloned.1.call-start = ((), (), s32[]{:S(2)}) async-start(), calls=%async_computation.1 | async-start | bytes 5603328 | tf_op jit(solution)/shard_map/all_gather | solution.py:118
  6.7 2.7 copy-start.3
  17.4 1.3 copy-start.2
  217.7 1.3 copy-start.1
  343.9 4.0 slice-start
  363.9 9.3 %copy-start.6 = (s32[64,4]{0,1:T(4,128)S(1)}, s32[64,4]{0,1:T(4,128)}, u32[]{:S(2)}) copy-start(s32[64,4]{0,1:T(4,128)} %param.7) | copy-start | bytes 3076
  366.2 31.7 %all-to-all-start = ((f32[16,1,16384]{2,1,0:T(1,128)}), f32[16,1,16384]{2,1,0:T(1,128)S(1)}, u32[]{:S(2)}, u32[]{:S(2)}) async-start(f32[16,1,16384]{2,1,0:T(1,128)} %reshape.539), calls=%async_computation | async-start | bytes 2097152 | tf_op jit(solution)/shard_map/all_to_all | solution.py:126
  409.2 6.9 %copy-start.4 = (f32[8,300,300]{2,1,0:T(8,128)S(1)}, f32[8,300,300]{2,1,0:T(8,128)}, u32[]{:S(2)}) copy-start(f32[8,300,300]{2,1,0:T(8,128)} %all-gather.2.cloned.1.call-done) | copy-start | bytes 8640004
  419.3 11.7 %collective-permute-start = (f32[64,3,300]{2,1,0:T(4,128)S(1)}, f32[64,3,300]{2,1,0:T(4,128)S(1)}, u32[]{:S(2)}, u32[]{:S(2)}) collective-permute-start(f32[64,3,300]{2,1,0:T(4,128)S(1)} %get-tuple-element.29), channel_id=1, source_target_pairs={{0,2},{2,4},{4,6},{6,8},{8,10},{10,12},{12,14},{14,16},{16,18},{18... | collective-permute-start | bytes 691208 | tf_op jit(solution)/shard_map/ppermute | solution.py:22
  421.5 19.6 %collective-permute-start.1 = (f32[64,3,300]{2,1,0:T(4,128)S(1)}, f32[64,3,300]{2,1,0:T(4,128)S(1)}, u32[]{:S(2)}, u32[]{:S(2)}) collective-permute-start(f32[64,3,300]{2,1,0:T(4,128)S(1)} %get-tuple-element.30), channel_id=1, source_target_pairs={{2,0},{4,2},{6,4},{8,6},{10,8},{12,10},{14,12},{16,14},{18,16},{20... | collective-permute-start | bytes 691208 | tf_op jit(solution)/shard_map/ppermute | solution.py:24
  441.1 5.0 %collective-permute-start.2 = (f32[3,10,300]{2,1,0:T(8,128)S(1)}, f32[3,10,300]{2,1,0:T(8,128)S(1)}, u32[]{:S(2)}, u32[]{:S(2)}) collective-permute-start(f32[3,10,300]{2,1,0:T(8,128)S(1)} %get-tuple-element.25), channel_id=1, source_target_pairs={{0,1},{2,3},{4,5},{6,7},{8,9},{10,11},{12,13},{14,15},{16,17},{18,... | collective-permute-start | bytes 108008 | tf_op jit(solution)/shard_map/ppermute | solution.py:22
  442.4 3.9 collective-permute-start.3
Sparse Core Ops, SparseCore 0:
  360.9 14.8 all-gather.1
where the time goes:
time: 470 us; the launch traced here: 465 us
  other arithmetic  336 us (71%)
  waiting for transfers between devices  39 us (8%)
  matrix products  34.2 us (7%)
  local copies, waits for them, and re-layouts  23.4 us (5%)
  starting transfers between devices  17.5 us (4%)
  between operations  14.6 us (3%)
    another operation x14, other arithmetic, invert(): factor = jnp.linalg.cholesky(matrix)  194 us
    another operation x9, other arithmetic, invert(): jax.scipy.linalg.cho_solve((factor, True), jnp.eye(DATES, dtype=jnp.float...  121 us
    all_to_all x1, waiting for transfers between devices, on_device(): lax.all_to_all(phases, 'ifg', split_axis=2, concat_axis=0, tiled=True)  24.5 us
    another operation x10, matrix products, invert(): jax.scipy.linalg.cho_solve((factor, True), jnp.eye(DATES, dtype=jnp.float...  14.5 us
    ppermute x2, waiting for transfers between devices, with_halo(): lax.ppermute(head, axis, [((i + 1) % count, i) for i in range(ends)])  10.3 us
    dot_general x8, matrix products, on_device(): jnp.einsum('pd,ed->pe', right_terms, inverse[member], precision=lax.Preci...  9.61 us
  transfers between devices with their start and end apart: 6, of which 4 were waited for; matrix products, arithmetic and copies ran while one was open for 4% of the time, Pallas kernels for 0%

commit v1 on v0

--- a/solution.py
+++ b/solution.py
@@ -123,7 +123,10 @@
         jnp.float32
     )
     weight_rows = class_weights.T
-    regrouped = lax.all_to_all(phases, "ifg", split_axis=2, concat_axis=0, tiled=True)
+    regrouped = jnp.concatenate(
+        lax.all_to_all(jnp.stack(jnp.split(phases, lax.axis_size("ifg"), axis=2)), "ifg", 0, 0),
+        axis=0,
+    )
     right_terms = date_terms(regrouped, incidence, weight_rows, onehot)
     solution = jnp.zeros((tile_rows * tile_cols, DATES), jnp.float32)
     for member in range(CLASSES):

time: 470 us -> 536 us (1.14)
  local copies, waits for them, and re-layouts: 23.4 us -> 86.8 us
    unnamed x22 -> x66, local copies, waits for them, and re-layouts: 8.7 us -> 53.9 us
    split x0 -> x1, local copies, waits for them, and re-layouts: none -> 15.2 us  [on_device(): jnp.split(phases, lax.axis_size('ifg'), axis=2)]
  transfers between devices with their start and end apart: 6 -> 6, of which waited for: 4 -> 3; matrix products, arithmetic and copies ran while one was open for 4% -> 15% of each run, Pallas kernels for 0% -> 0%
where the time goes in v1:
time: 536 us; the launch traced here: 530 us
  other arithmetic  337 us (63%)
  local copies, waits for them, and re-layouts  86.8 us (16%)
  waiting for transfers between devices  38.4 us (7%)
  matrix products  35 us (7%)
  starting transfers between devices  17.8 us (3%)
  between operations  14.4 us (3%)
    another operation x14, other arithmetic, invert(): factor = jnp.linalg.cholesky(matrix)  194 us
    another operation x9, other arithmetic, invert(): jax.scipy.linalg.cho_solve((factor, True), jnp.eye(DATES, dtype=jnp.float...  122 us
    unnamed x66, local copies, waits for them, and re-layouts  53.9 us
    all_to_all x1, waiting for transfers between devices, on_device(): lax.all_to_all(jnp.stack(jnp.split(phases, lax.axis_size('ifg'), axis=2))...  24.6 us
    split x1, local copies, waits for them, and re-layouts, on_device(): jnp.split(phases, lax.axis_size('ifg'), axis=2)  15.2 us
    another operation x10, matrix products, invert(): jax.scipy.linalg.cho_solve((factor, True), jnp.eye(DATES, dtype=jnp.float...  14.5 us
    ppermute x2, waiting for transfers between devices, with_halo(): lax.ppermute(head, axis, [((i + 1) % count, i) for i in range(ends)])  12.6 us
  transfers between devices with their start and end apart: 6, of which 3 were waited for; matrix products, arithmetic and copies ran while one was open for 15% of the time, Pallas kernels for 0%

profile of v1, /device:TPU:13, one launch (start us, length us, event | category | flops | bytes accessed | tf_op | source)
XLA Modules:
  0.0 529.9 jit_solution(12543109315003079016)
XLA Ops:
  7.2 2.2 bitcast_add_fusion
  14.4 4.5 fusion.2
  20.2 46.9 %custom-call.29 = f32[4,128,128]{2,1,0:T(8,128)S(1)} custom-call(f32[4,128,128]{2,1,0:T(8,128)S(1)} %cholesky.205), custom_call_target="Cholesky" | custom-call | tf_op jit(solution)/shard_map/vmap(jit(cholesky))/cholesky | solution.py:78
  67.2 39.9 %custom-call.30 = f32[4,1,128,128]{2,3,1,0:T(8,128)} custom-call(f32[4,1,128,128]{3,2,1,0:T(8,128)S(1)} %select_bitcast_fusion.1), custom_call_target="InvertDiagBlocksLowerTriangular" | custom-call | tf_op jit(solution)/shard_map/vmap(jit(cholesky))/cholesky | solution.py:78
  108.7 1.7 convolution_subtract_fusion.3
  111.1 48.5 %custom-call.31 = f32[4,128,128]{2,1,0:T(8,128)} custom-call(f32[4,128,128]{2,1,0:T(8,128)} %cholesky.209), custom_call_target="Cholesky" | custom-call | tf_op jit(solution)/shard_map/vmap(jit(cholesky))/cholesky | solution.py:78
  159.6 1.7 select_reduce_fusion
  161.3 40.1 %custom-call.32 = f32[4,1,128,128]{2,3,1,0:T(8,128)S(1)} custom-call(f32[4,1,128,128]{3,2,1,0:T(8,128)} %get-tuple-element.47), custom_call_target="InvertDiagBlocksLowerTriangular" | custom-call | tf_op jit(solution)/shard_map/vmap(jit(cholesky))/cholesky | solution.py:78
  203.0 16.1 %custom-call.33 = f32[4,44,44]{2,1,0:T(8,128)S(1)} custom-call(f32[4,44,44]{2,1,0:T(8,128)S(1)} %convolution_subtract_fusion.4), custom_call_target="Cholesky" | custom-call | tf_op jit(solution)/shard_map/vmap(jit(cholesky))/cholesky | solution.py:78
  220.4 1.8 select_select_fusion
  222.3 3.9 while.1
  226.5 118.9 %custom-call.34 = f32[4,3,128,128]{2,3,1,0:T(8,128)} custom-call(f32[4,3,128,128]{3,2,1,0:T(8,128)S(1)} %pad_maximum_fusion.2), custom_call_target="InvertDiagBlocksLowerTriangular" | custom-call | tf_op jit(solution)/shard_map/vmap(jit(_cho_solve))/triangular_solve | solution.py:79
  345.5 1.6 fusion.72
  347.8 1.6 fusion.81
  353.7 2.3 convolution_subtract_fusion.1
  356.0 1.6 fusion.80
  358.9 1.6 fusion.79
  361.9 3.0 copy.118
  364.9 15.2 %fusion.105 = (f32[64,64,4]{2,1,0:T(8,128)}, f32[64,64,4]{2,1,0:T(8,128)}, f32[64,64,4]{2,1,0:T(8,128)}, f32[64,64,4]{2,1,0:T(8,128)}, f32[64,64,4]{2,1,0:T(8,12...) fusion(f32[64,64,64]{2,1,0:T(8,128)S(1)} %copy-done.1), kind=kLoop, calls=%fused_computation.271 | loop fusion | bytes 2097152 | tf_op jit(solution)/shard_map/split | solution.py:127
  380.1 2.3 copy.138
  383.1 3.1 copy.139
  386.2 2.9 copy.140
  390.4 3.1 copy.142
  393.5 2.9 copy.143
  397.1 2.5 copy.145
  399.6 2.3 copy.146
  402.6 2.5 copy.148
  405.1 2.3 copy.149
  408.1 2.5 copy.151
  410.6 2.3 copy.152
  413.6 1.6 bitcast_dynamic-update-slice_fusion.15
  419.8 1.6 bitcast_dynamic-update-slice_fusion.11
  428.0 3.5 reshape.534
  431.4 6.6 %all-to-all-start = ((f32[16,1,16384]{2,1,0:T(1,128)}), f32[16,1,16384]{2,1,0:T(1,128)S(1)}, u32[]{:S(2)}, u32[]{:S(2)}) async-start(f32[16,1,16384]{2,1,0:T(1,128)} %reshape.534), calls=%async_computation | async-start | bytes 2097152 | tf_op jit(solution)/shard_map/all_to_all | solution.py:127
  438.3 24.6 %all-to-all-done = f32[16,1,16384]{2,1,0:T(1,128)S(1)} async-done(((f32[16,1,16384]{2,1,0:T(1,128)}), f32[16,1,16384]{2,1,0:T(1,128)S(1)}, u32[]{:S(2)}, u32[]{:S(2)}) %all-to-all-start) | async-done | bytes 1048608 | tf_op jit(solution)/shard_map/all_to_all | solution.py:127
  463.4 3.1 reduce.18
  467.4 2.7 copy.99
  470.1 2.2 reshape_reshape.3
  474.4 1.8 convolution_multiply_fusion
  476.2 1.7 convolution_multiply_fusion.1
  477.9 1.7 convolution_multiply_fusion.2
  479.6 1.7 convolution_multiply_fusion.3
  484.5 1.9 collective-permute-start.1
  486.4 3.4 collective-permute-start
  491.1 12.6 %collective-permute-done.1 = f32[64,3,300]{2,1,0:T(4,128)S(1)} collective-permute-done((f32[64,3,300]{2,1,0:T(4,128)S(1)}, f32[64,3,300]{2,1,0:T(4,128)S(1)}, u32[]{:S(2)}, u32[]{:S(2)}) %collective-permute-start.1) | collective-permute-done | bytes 230432 | tf_op jit(solution)/shard_map/ppermute | solution.py:24
  503.7 4.6 collective-permute-start.3
  511.9 5.2 fusion.56
  517.2 5.7 %fusion.63 = f32[64,4,300]{2,1,0:T(4,128)} fusion(f32[64,4,300]{2,1,0:T(4,128)S(1)} %reshape.511, f32[70,4,300]{2,1,0:T(4,128)S(1)} %fusion.56, f32[]{:T(128)} %bitcast.53, f32[]{:T(128)} %bitcast.52, f32[]{:T(128)} %bitcast.51, f32[]{:T(128)} %bitcast.50, f32[]{:T(128)} %bitcast.49, f32[]{:T(128)} %bitcast.48, f32[]{:T(128)} %bitcast.47), kind=kLoop, calls=%fused_computation.157 | loop fusion | flops 1075200 | bytes 2764828 | tf_op jit(solution)/shard_map/sub | solution.py:142
  (148 shorter events, 51.3 us)
Async XLA Ops:
  6.5 3.4 copy-start
  6.5 0.7 copy-start.12
  6.5 467.8 %all-gather.2.cloned.1.call-start = ((), (), s32[]{:S(2)}) async-start(), calls=%async_computation.1 | async-start | bytes 5603328 | tf_op jit(solution)/shard_map/all_gather | solution.py:118
  6.6 2.9 copy-start.10
  18.9 1.3 copy-start.9
  219.2 1.3 copy-start.7
  345.5 4.0 slice-start
  349.5 2.7 copy-start.8
  361.9 3.0 copy-start.1
  383.1 6.0 %copy-start.6 = (f32[64,64,4]{2,1,0:T(8,128)S(1)}, f32[64,64,4]{2,1,0:T(8,128)}, u32[]{:S(2)}) copy-start(f32[64,64,4]{2,1,0:T(8,128)} %get-tuple-element.37) | copy-start | bytes 196612
  390.4 6.0 %copy-start.5 = (f32[64,64,4]{2,1,0:T(8,128)S(1)}, f32[64,64,4]{2,1,0:T(8,128)}, u32[]{:S(2)}) copy-start(f32[64,64,4]{2,1,0:T(8,128)} %get-tuple-element.34) | copy-start | bytes 196612
  397.1 4.8 copy-start.4
  402.6 4.8 copy-start.3
  408.1 4.8 copy-start.2
  428.0 10.1 %copy-start.13 = (s32[64,4]{0,1:T(4,128)S(1)}, s32[64,4]{0,1:T(4,128)}, u32[]{:S(2)}) copy-start(s32[64,4]{0,1:T(4,128)} %param.7) | copy-start | bytes 3076
  431.4 31.4 %all-to-all-start = ((f32[16,1,16384]{2,1,0:T(1,128)}), f32[16,1,16384]{2,1,0:T(1,128)S(1)}, u32[]{:S(2)}, u32[]{:S(2)}) async-start(f32[16,1,16384]{2,1,0:T(1,128)} %reshape.534), calls=%async_computation | async-start | bytes 2097152 | tf_op jit(solution)/shard_map/all_to_all | solution.py:127
  474.4 6.9 %copy-start.11 = (f32[8,300,300]{2,1,0:T(8,128)S(1)}, f32[8,300,300]{2,1,0:T(8,128)}, u32[]{:S(2)}) copy-start(f32[8,300,300]{2,1,0:T(8,128)} %all-gather.2.cloned.1.call-done) | copy-start | bytes 8640004
  484.5 19.2 %collective-permute-start.1 = (f32[64,3,300]{2,1,0:T(4,128)S(1)}, f32[64,3,300]{2,1,0:T(4,128)S(1)}, u32[]{:S(2)}, u32[]{:S(2)}) collective-permute-start(f32[64,3,300]{2,1,0:T(4,128)S(1)} %get-tuple-element.46), channel_id=1, source_target_pairs={{2,0},{4,2},{6,4},{8,6},{10,8},{12,10},{14,12},{16,14},{18,16},{20... | collective-permute-start | bytes 691208 | tf_op jit(solution)/shard_map/ppermute | solution.py:24
  486.4 17.3 %collective-permute-start = (f32[64,3,300]{2,1,0:T(4,128)S(1)}, f32[64,3,300]{2,1,0:T(4,128)S(1)}, u32[]{:S(2)}, u32[]{:S(2)}) collective-permute-start(f32[64,3,300]{2,1,0:T(4,128)S(1)} %get-tuple-element.45), channel_id=1, source_target_pairs={{0,2},{2,4},{4,6},{6,8},{8,10},{10,12},{12,14},{14,16},{16,18},{18... | collective-permute-start | bytes 691208 | tf_op jit(solution)/shard_map/ppermute | solution.py:22
  503.7 6.6 %collective-permute-start.3 = (f32[3,10,300]{2,1,0:T(8,128)S(1)}, f32[3,10,300]{2,1,0:T(8,128)S(1)}, u32[]{:S(2)}, u32[]{:S(2)}) collective-permute-start(f32[3,10,300]{2,1,0:T(8,128)S(1)} %get-tuple-element.42), channel_id=1, source_target_pairs={{1,0},{3,2},{5,4},{7,6},{9,8},{11,10},{13,12},{15,14},{17,16},{19,... | collective-permute-start | bytes 108008 | tf_op jit(solution)/shard_map/ppermute | solution.py:24
  508.3 3.2 collective-permute-start.2
Sparse Core Ops, SparseCore 0:
  365.0 14.8 all-gather.1
